TPU v7x, 128 devices: a whole 4x4x4 slice. The times are simulated.
128 devices in a mesh: gx: 32 (over y, z, core), gy: 4 (over x).
Axes of the slice: x: 4, y: 4, z: 4, core: 2. Of those that a mesh axis runs over, the one named last changes fastest.
Arguments:
- latent: bfloat16 [256, 16, 128, 128], P('gx', 'gy'), may hold values from -6 to 6
- migration: int32 [32, 4, 8, 64], P('gx', 'gy'), may hold values from 0 to 4095, as said below
- tile_target: int32 [32, 4, 128], P('gx', 'gy'), may hold values from 0 to 31
- tile_offset: int32 [32, 4, 128], P('gx', 'gy'), may hold values from 0 to 8
- tile_count: int32 [32, 4], P('gx', 'gy'), may hold values from 64 to 128, as said below
- edge_sender: int32 [32, 4, 128, 128], P('gx', 'gy'), may hold values from 0 to 127
- edge_target: int32 [32, 4, 128, 128], P('gx', 'gy'), may hold values from 0 to 127
- send_weight: bfloat16 [3, 128, 128], replicated, may hold values from -0.375 to 0.375
- receive_weight: bfloat16 [3, 128, 128], replicated, may hold values from -0.375 to 0.375
- edge_bias: float32 [3, 128], replicated, may hold values from -3 to 3
- edge_weight: bfloat16 [3, 128, 128], replicated, may hold values from -0.5 to 0.5
- edge_gain: float32 [3, 128], replicated, may hold values from 0.5 to 2
- node_weight: bfloat16 [3, 128, 128], replicated, may hold values from -0.375 to 0.375
- aggregate_weight: bfloat16 [3, 128, 128], replicated, may hold values from -0.1875 to 0.1875
- node_bias: float32 [3, 128], replicated, may hold values from -3 to 3
- output_weight: bfloat16 [3, 128, 128], replicated, may hold values from -0.5 to 0.5
- node_gain: float32 [3, 128], replicated, may hold values from 0.5 to 2
Outputs:
- updated: bfloat16 [256, 16, 128, 128], P('gx', 'gy')
Inputs may be any that keep to these rules, and one draw needn't show every extreme that they name: `migration`: within each device the 512 entries are distinct rows of 0 to 4095. `tile_count`: some device has all 128 tiles live.
All inputs are finite; a program needn't handle non-finite values.
Results may differ from a plain program's by a relative error of at most 0.009.
Values may be sent and summed in bfloat16 or wider, within the bound.
A program may use at most 128 MiB of HBM per device.

v0:
```python
import jax
import jax.numpy as jnp
from jax import lax
from jax.experimental import pallas as pl
from jax.experimental.pallas import tpu as pltpu
from jax.sharding import PartitionSpec as P

DIRECTIONS = ((-1, -1), (-1, 0), (-1, 1), (0, -1), (0, 1), (1, -1), (1, 0), (1, 1))
MESH = pl.DeviceIdType.MESH
F32 = jnp.float32
BF16 = jnp.bfloat16
LANES = 128
GROUP = 16
LAYERS = 3


def dot(left, right):
    return jnp.dot(left, right, preferred_element_type=F32)


def turned(identity, block):
    return lax.dot_general(identity, block, (((1,), (1,)), ((), ())), preferred_element_type=F32)


def kernel(
    latent, mig_s, mig_v, target, offset, count, senders, receivers,
    send_w, recv_w, edge_b, edge_w, edge_g, node_w, agg_w, node_b, out_w, node_g,
    out_ref,
    lat, lat32, stage, parcels, arrived, arrived_t, mig_hot,
    es, er, hot, hot_n, ps0, ps1, ps2, pr, sums, state,
    w_sr, w_edge, w_node, w_out, columns, raw, plan_v, plan,
    in_sem, plan_sem, mig_send, mig_recv, halo_send, halo_recv, out_sem,
):
    bins_x, bins_y = out_ref.shape[0], out_ref.shape[1]
    tiles = es.shape[0]
    across = bins_x + 2
    tables = (ps0, ps1, ps2)
    a, b = lax.axis_index("gx"), lax.axis_index("gy")
    count_a, count_b = lax.axis_size("gx"), lax.axis_size("gy")

    def neighbour(step_x, step_y):
        return (lax.rem(a + step_x + count_a, count_a), lax.rem(b + step_y + count_b, count_b))

    lat_copy = pltpu.make_async_copy(latent, lat, in_sem.at[0])
    lat_copy.start()
    loads = [
        pltpu.make_async_copy(source, raw.at[which], in_sem.at[1 + which])
        for which, source in enumerate((send_w, recv_w, edge_w, node_w, agg_w, out_w))
    ]
    edge_loads = [
        pltpu.make_async_copy(senders.at[0, 0], es, in_sem.at[7]),
        pltpu.make_async_copy(receivers.at[0, 0], er, in_sem.at[8]),
    ]
    for copy in loads + edge_loads:
        copy.start()

    barrier = pltpu.get_barrier_semaphore()
    for step_x, step_y in DIRECTIONS:
        pl.semaphore_signal(
            barrier, inc=1, device_id=neighbour(step_x, step_y), device_id_type=MESH
        )

    lat_copy.wait()

    def widen(n, _):
        lat32[pl.ds(n * LANES, LANES), :] = lat[n // bins_y, n % bins_y].astype(F32)
        return 0

    lax.fori_loop(0, bins_x * bins_y, widen, 0, unroll=4)

    pl.semaphore_wait(barrier, 8)

    mig = mig_s.shape[3]
    mig_copies = []
    for which, (step_x, step_y) in enumerate(DIRECTIONS):

        def pick(m, _, which=which):
            stage[pl.ds(m, 1), :] = lat32[pl.ds(mig_s[0, 0, which, m], 1), :]
            return 0

        lax.fori_loop(0, mig, pick, 0, unroll=16)
        parcels[which] = stage[...].astype(BF16)
        copy = pltpu.make_async_remote_copy(
            src_ref=parcels.at[which],
            dst_ref=arrived.at[7 - which],
            send_sem=mig_send.at[which],
            recv_sem=mig_recv.at[7 - which],
            device_id=neighbour(step_x, step_y),
            device_id_type=MESH,
        )
        copy.start()
        mig_copies.append(copy)

    sub = lax.broadcasted_iota(jnp.int32, (LANES, LANES), 0)
    lane = lax.broadcasted_iota(jnp.int32, (LANES, LANES), 1)
    identity = jnp.where(sub == lane, 1.0, 0.0).astype(BF16)

    def spread(row):
        return jnp.transpose(jnp.broadcast_to(row, (LANES, LANES)))

    for quarter in range(4):
        row = jnp.concatenate(
            [mig_v[0, 0, 2 * quarter : 2 * quarter + 1, :], mig_v[0, 0, 2 * quarter + 1 : 2 * quarter + 2, :]],
            axis=1,
        ).astype(F32)
        index = spread(row).astype(jnp.int32)

        def mark(n, _, index=index, quarter=quarter):
            mig_hot[n, quarter * LANES : (quarter + 1) * LANES, :] = jnp.where(
                index - n * LANES == lane, 1.0, 0.0
            ).astype(BF16)
            return 0

        lax.fori_loop(0, bins_x * bins_y, mark, 0, unroll=4)

    def turn(n, _):
        state[n] = turned(identity, lat[n // bins_y, n % bins_y]).astype(BF16)
        return 0

    lax.fori_loop(0, bins_x * bins_y, turn, 0, unroll=8)

    lane_row = lax.broadcasted_iota(jnp.int32, (1, LANES), 1)
    bin_row = target[0, 0:1, :]
    off_row = offset[0, 0:1, :]
    step_row = jnp.right_shift(off_row * 11, 5)
    side_row = off_row - 3 * step_row
    sender_row = (jnp.bitwise_and(bin_row, 3) + side_row) * across + (
        jnp.right_shift(bin_row, 2) + step_row
    )
    key_row = bin_row * LANES + lane_row
    key_col = spread(key_row)
    packed_col = spread((sender_row * 32 + bin_row) * LANES + lane_row)
    rank = jnp.sum(
        jnp.where(jnp.broadcast_to(key_row, (LANES, LANES)) < key_col, 1, 0),
        axis=1,
        keepdims=True,
    )
    ordered = jnp.sum(jnp.where(rank == lane, packed_col, 0), axis=0, keepdims=True)
    tile_of = jnp.bitwise_and(ordered, LANES - 1)
    bin_of = jnp.bitwise_and(jnp.right_shift(ordered, 7), 31)
    sender_of = jnp.clip(jnp.right_shift(ordered, 12), 0, across * (bins_y + 2) - 1)
    before = pltpu.roll(bin_of, 1, 1)
    goes_on = jnp.where(jnp.logical_and(before == bin_of, lane_row > 0), 1, 0)
    live = jnp.where(tile_of < count[0, 0], 1, 0)
    bin_col = jnp.right_shift(key_col, 7)
    up_to = jnp.sum(jnp.where(bin_col <= lane, 1, 0), axis=0, keepdims=True)
    own = jnp.sum(jnp.where(bin_col == lane, 1, 0), axis=0, keepdims=True)
    last = jnp.clip(jnp.where(own > 0, up_to - 1, tiles), 0, tiles)
    plan_v[...] = jnp.concatenate(
        [tile_of, sender_of, bin_of, goes_on, live, last, last, last], axis=0
    )
    plan_copy = pltpu.make_async_copy(plan_v, plan, plan_sem)
    plan_copy.start()
    sums[tiles] = jnp.zeros((LANES, LANES), BF16)

    for copy in loads:
        copy.wait()
    for layer in range(LAYERS):
        w_sr[layer, :LANES, :] = turned(identity, raw[0, layer]).astype(BF16)
        w_sr[layer, LANES:, :] = turned(identity, raw[1, layer]).astype(BF16)
        for which, place in ((2, w_edge), (5, w_out)):
            full = turned(identity, raw[which, layer])
            place[layer] = (full - jnp.mean(full, axis=0, keepdims=True)).astype(BF16)
        w_node[layer, :, :LANES] = turned(identity, raw[3, layer]).astype(BF16)
        w_node[layer, :, LANES:] = (
            turned(identity, raw[4, layer]) * edge_g[layer : layer + 1, :]
        ).astype(BF16)
        columns[layer, 0] = spread(edge_b[layer : layer + 1, :])
        columns[layer, 1] = spread(node_b[layer : layer + 1, :])
        columns[layer, 2] = spread(node_g[layer : layer + 1, :])

    def place_tables(layer, cells, values):
        both = dot(w_sr[layer], values)
        for n, (i, j) in enumerate(cells):
            part = both[:, n * LANES : (n + 1) * LANES]
            tables[layer][(j + 1) * across + i + 1] = part[:LANES].astype(BF16)
            pr[i * bins_y + j] = (part[LANES:] + columns[layer, 0]).astype(BF16)

    def remote(layer, source, place, rows, slot, device):
        return pltpu.make_async_remote_copy(
            src_ref=tables[layer].at[pl.ds(source, rows)],
            dst_ref=tables[layer].at[pl.ds(place, rows)],
            send_sem=halo_send.at[layer, slot],
            recv_sem=halo_recv.at[layer, slot],
            device_id=device,
            device_id_type=MESH,
        )

    pairs = bins_x // 2

    def column_copies(layer, n):
        left = remote(
            layer, across + 1 + 2 * n, (bins_y + 1) * across + 1 + 2 * n, 2, n, neighbour(0, -1)
        )
        right = remote(
            layer, bins_y * across + 1 + 2 * n, 1 + 2 * n, 2, pairs + n, neighbour(0, 1)
        )
        return left, right

    def other_copies(layer):
        copies = []
        slot = 2 * pairs
        for step_x, step_y in ((-1, -1), (-1, 1), (1, -1), (1, 1)):
            source = (1 if step_y < 0 else bins_y) * across + (1 if step_x < 0 else bins_x)
            place = (bins_y + 1 if step_y < 0 else 0) * across + (
                bins_x + 1 if step_x < 0 else 0
            )
            copies.append(remote(layer, source, place, 1, slot, neighbour(step_x, step_y)))
            slot += 1
        for step_x in (-1, 1):
            for j in range(bins_y):
                source = (j + 1) * across + (1 if step_x < 0 else bins_x)
                place = (j + 1) * across + (bins_x + 1 if step_x < 0 else 0)
                copies.append(remote(layer, source, place, 1, slot, neighbour(step_x, 0)))
                slot += 1
        return copies

    def exchange(layer, renew):
        def outer(n, _):
            cells = [(2 * n, 0), (2 * n + 1, 0), (2 * n, bins_y - 1), (2 * n + 1, bins_y - 1)]
            place_tables(layer, cells, renew(cells))
            for copy in column_copies(layer, n):
                copy.start()
            return 0

        lax.fori_loop(0, pairs, outer, 0)
        corners = other_copies(layer)
        for copy in corners[:4]:
            copy.start()

        def inner(n, _):
            cells = [(2 * n, 1), (2 * n + 1, 1), (2 * n, 2), (2 * n + 1, 2)]
            place_tables(layer, cells, renew(cells))
            return 0

        lax.fori_loop(0, pairs, inner, 0)
        for copy in corners[4:]:
            copy.start()

    def finish_exchange(layer):
        for copy in other_copies(layer):
            copy.wait()
        for n in range(pairs):
            for copy in column_copies(layer, n):
                copy.wait()

    for copy in mig_copies:
        copy.wait()
    for quarter in range(4):
        block = jnp.concatenate([arrived[2 * quarter], arrived[2 * quarter + 1]], axis=0)
        arrived_t[:LANES, quarter * LANES : (quarter + 1) * LANES] = turned(
            identity, block
        ).astype(BF16)
    arrived_t[LANES:, :] = jnp.ones((16, 4 * LANES), BF16)

    def settle(cells):
        values = []
        for i, j in cells:
            n = i * bins_y + j
            placed = dot(arrived_t[...], mig_hot[n])
            new = jnp.where(
                placed[LANES : LANES + 1] > 0.5, placed[:LANES], state[n].astype(F32)
            ).astype(BF16)
            state[n] = new
            values.append(new)
        return jnp.concatenate(values, axis=1)

    exchange(0, settle)

    plan_copy.wait()
    for copy in edge_loads:
        copy.wait()

    def mark_tile(p, _):
        t = plan[0, p]
        from_row = es[pl.ds(t, 1), :]
        to_row = er[pl.ds(t, 1), :]
        hot[p, :LANES, :] = jnp.where(sub == from_row, 1.0, 0.0).astype(BF16)
        to_hot = jnp.where(sub == to_row, 1.0, 0.0).astype(BF16)
        hot[p, LANES:, :] = to_hot
        hot_n[p] = (turned(identity, to_hot) * plan[4, p].astype(F32)).astype(BF16)
        return 0

    lax.fori_loop(0, tiles, mark_tile, 0, unroll=8)

    def messages(layer):
        table = tables[layer]

        def group(q, total):
            hidden = []
            for g in range(GROUP):
                p = q * GROUP + g
                both = jnp.concatenate([table[plan[1, p]], pr[plan[2, p]]], axis=1)
                hidden.append(jnp.maximum(dot(both, hot[p]), 0.0).astype(BF16))
            sent = []
            for g in range(0, GROUP, 2):
                pair = dot(w_edge[layer], jnp.concatenate(hidden[g : g + 2], axis=1))
                var = jnp.mean(pair * pair, axis=0, keepdims=True)
                pair = (pair * lax.rsqrt(var + 1e-5)).astype(BF16)
                sent += [pair[:, :LANES], pair[:, LANES:]]
            for g in range(GROUP):
                p = q * GROUP + g
                total = total * plan[3, p].astype(F32) + dot(sent[g], hot_n[p])
                sums[p] = total.astype(BF16)
            return total

        lax.fori_loop(0, tiles // GROUP, group, jnp.zeros((LANES, LANES), F32))

    def node(layer):
        def renew(cells):
            old = jnp.concatenate([state[i * bins_y + j] for i, j in cells], axis=1)
            summed = jnp.concatenate(
                [sums[plan[5, i * bins_y + j]] for i, j in cells], axis=1
            )
            many = len(cells)
            bias = jnp.concatenate([columns[layer, 1]] * many, axis=1)
            gain = jnp.concatenate([columns[layer, 2]] * many, axis=1)
            hidden = dot(w_node[layer], jnp.concatenate([old, summed], axis=0)) + bias
            hidden = jnp.maximum(hidden, 0.0).astype(BF16)
            z = dot(w_out[layer], hidden)
            var = jnp.mean(z * z, axis=0, keepdims=True)
            new = (old.astype(F32) + z * lax.rsqrt(var + 1e-5) * gain).astype(BF16)
            if layer < LAYERS - 1:
                for n, (i, j) in enumerate(cells):
                    state[i * bins_y + j] = new[:, n * LANES : (n + 1) * LANES]
            return new

        return renew

    for layer in range(LAYERS):
        finish_exchange(layer)
        messages(layer)
        if layer < LAYERS - 1:
            exchange(layer + 1, node(layer))
        else:
            renew = node(layer)

            def final(n, _):
                cells = [(n, j) for j in range(bins_y)]
                new = renew(cells)
                for j in range(bins_y):
                    lat[n, j] = turned(identity, new[:, j * LANES : (j + 1) * LANES]).astype(BF16)
                pltpu.make_async_copy(lat.at[n], out_ref.at[n], out_sem.at[n]).start()
                return 0

            lax.fori_loop(0, bins_x, final, 0)
            for n in range(bins_x):
                pltpu.make_async_copy(lat.at[n], out_ref.at[n], out_sem.at[n]).wait()


def body(*arguments):
    latent, migration, tile_target, tile_offset, tile_count = arguments[:5]
    bins_x, bins_y, slots, features = latent.shape
    tiles = tile_target.shape[2]
    mig = migration.shape[3]
    cells = bins_x * bins_y
    table = (bins_x + 2) * (bins_y + 2)
    hbm = pl.BlockSpec(memory_space=pl.ANY)
    vmem = pl.BlockSpec(memory_space=pltpu.VMEM)
    smem = pl.BlockSpec(memory_space=pltpu.SMEM)
    block = (LANES, LANES)
    halos = 2 * (bins_x // 2) + 4 + 2 * bins_y
    dma = pltpu.SemaphoreType.DMA
    return pl.pallas_call(
        kernel,
        out_shape=jax.ShapeDtypeStruct(latent.shape, latent.dtype),
        in_specs=[
            hbm, smem, vmem, vmem, vmem, smem, hbm, hbm,
            hbm, hbm, vmem, hbm, vmem, hbm, hbm, vmem, hbm, vmem,
        ],
        out_specs=hbm,
        scratch_shapes=[
            pltpu.VMEM(latent.shape, BF16),
            pltpu.VMEM((cells * slots, features), F32),
            pltpu.VMEM((mig, features), F32),
            pltpu.VMEM((8, mig, features), BF16),
            pltpu.VMEM((8, mig, features), BF16),
            pltpu.VMEM((LANES + 16, 8 * mig), BF16),
            pltpu.VMEM((cells, 8 * mig, LANES), BF16),
            pltpu.VMEM((tiles, LANES), jnp.int32),
            pltpu.VMEM((tiles, LANES), jnp.int32),
            pltpu.VMEM((tiles, 2 * LANES, LANES), BF16),
            pltpu.VMEM((tiles,) + block, BF16),
            pltpu.VMEM((table,) + block, BF16),
            pltpu.VMEM((table,) + block, BF16),
            pltpu.VMEM((table,) + block, BF16),
            pltpu.VMEM((cells,) + block, BF16),
            pltpu.VMEM((tiles + 1,) + block, BF16),
            pltpu.VMEM((cells,) + block, BF16),
            pltpu.VMEM((LAYERS, 2 * LANES, LANES), BF16),
            pltpu.VMEM((LAYERS,) + block, BF16),
            pltpu.VMEM((LAYERS, LANES, 2 * LANES), BF16),
            pltpu.VMEM((LAYERS,) + block, BF16),
            pltpu.VMEM((LAYERS, 3) + block, F32),
            pltpu.VMEM((6, LAYERS) + block, BF16),
            pltpu.VMEM((8, LANES), jnp.int32),
            pltpu.SMEM((8, LANES), jnp.int32),
            dma((9,)),
            dma,
            dma((8,)),
            dma((8,)),
            dma((LAYERS, halos)),
            dma((LAYERS, halos)),
            dma((bins_x,)),
        ],
        compiler_params=pltpu.CompilerParams(
            collective_id=0, has_side_effects=True, vmem_limit_bytes=56 << 20
        ),
        name="particles",
    )(arguments[0], migration, *arguments[1:])


def solution(mesh):
    split = P("gx", "gy")
    in_specs = (split,) * 7 + (P(),) * 10
    return jax.shard_map(
        body, mesh=mesh, in_specs=in_specs, out_specs=split, check_vma=False
    )
```

profile of v0, /device:TPU:0, one launch (start us, length us, event | category | flops | bytes accessed | tf_op | source)
XLA Modules:
  0.0 75.2 jit_solution(18097139613788702907)
XLA Ops:
  0.7 72.3 %particles.1 = bf16[8,4,128,128]{3,2,1,0:T(8,128)(2,1)} custom-call(bf16[8,4,128,128]{3,2,1,0:T(8,128)(2,1)} %latent.1, s32[1,1,8,64]{3,2,1,0:T(8,128)} %mig_v.1, s32[1,1,8,64]{3,2,1,0:T(8,128)} %mig_v.1, s32[1,1,128]{2,1,0:T(1,128)} %target.1, s32[1,1,128]{2,1,0:T(1,128)} %offset.1, s32[1,1]{1,0:T(1,128)S(6)} %copy.19.count, s32[1,1,128,128]{3,2,1,0:T(8,128)} %senders.1, ...), custom_call_target="tpu_custom_call" | custom-call | tf_op jit(solution)/shard_map/particles/pallas_call | solution.py:364
  72.9 2.3 %copy.20 = bf16[8,4,128,128]{3,2,1,0:T(8,128)(2,1)} copy(bf16[8,4,128,128]{3,2,1,0:T(8,128)(2,1)} %particles.1) | data formatting | bytes 2097152
where the time goes:
time: 75.4 us; the launch traced here: 75.2 us
  Pallas kernels  72.3 us (96%)
  local copies, waits for them, and re-layouts  2.31 us (3%)
    pallas_call x1, Pallas kernels, body(): pl.pallas_call(kernel, out_shape=jax.ShapeDtypeStruct(latent.shape, laten...  72.3 us
    unnamed x1, local copies, waits for them, and re-layouts  2.31 us

commit v1 on v0

--- a/solution.py
+++ b/solution.py
@@ -10,8 +10,10 @@
 F32 = jnp.float32
 BF16 = jnp.bfloat16
 LANES = 128
-GROUP = 16
+GROUP = 32
 LAYERS = 3
+EARLY = 64
+FINAL = 4
 
 
 def dot(left, right):
@@ -27,7 +29,7 @@
     send_w, recv_w, edge_b, edge_w, edge_g, node_w, agg_w, node_b, out_w, node_g,
     out_ref,
     lat, lat32, stage, parcels, arrived, arrived_t, mig_hot,
-    es, er, hot, hot_n, ps0, ps1, ps2, pr, sums, state,
+    es, er, hot, hot_n, to_rows, ps0, ps1, ps2, pr, sums, state,
     w_sr, w_edge, w_node, w_out, columns, raw, plan_v, plan,
     in_sem, plan_sem, mig_send, mig_recv, halo_send, halo_recv, out_sem,
 ):
@@ -124,7 +126,7 @@
     off_row = offset[0, 0:1, :]
     step_row = jnp.right_shift(off_row * 11, 5)
     side_row = off_row - 3 * step_row
-    sender_row = (jnp.bitwise_and(bin_row, 3) + side_row) * across + (
+    sender_row = (jnp.bitwise_and(bin_row, 3) + side_row) * 16 + (
         jnp.right_shift(bin_row, 2) + step_row
     )
     key_row = bin_row * LANES + lane_row
@@ -138,7 +140,8 @@
     ordered = jnp.sum(jnp.where(rank == lane, packed_col, 0), axis=0, keepdims=True)
     tile_of = jnp.bitwise_and(ordered, LANES - 1)
     bin_of = jnp.bitwise_and(jnp.right_shift(ordered, 7), 31)
-    sender_of = jnp.clip(jnp.right_shift(ordered, 12), 0, across * (bins_y + 2) - 1)
+    sender_y = jnp.clip(jnp.right_shift(ordered, 16), 0, bins_y + 1)
+    sender_x = jnp.clip(jnp.bitwise_and(jnp.right_shift(ordered, 12), 15), 0, across - 1)
     before = pltpu.roll(bin_of, 1, 1)
     goes_on = jnp.where(jnp.logical_and(before == bin_of, lane_row > 0), 1, 0)
     live = jnp.where(tile_of < count[0, 0], 1, 0)
@@ -147,7 +150,7 @@
     own = jnp.sum(jnp.where(bin_col == lane, 1, 0), axis=0, keepdims=True)
     last = jnp.clip(jnp.where(own > 0, up_to - 1, tiles), 0, tiles)
     plan_v[...] = jnp.concatenate(
-        [tile_of, sender_of, bin_of, goes_on, live, last, last, last], axis=0
+        [tile_of, sender_y, bin_of, goes_on, live, last, sender_x, last], axis=0
     )
     plan_copy = pltpu.make_async_copy(plan_v, plan, plan_sem)
     plan_copy.start()
@@ -173,76 +176,82 @@
         both = dot(w_sr[layer], values)
         for n, (i, j) in enumerate(cells):
             part = both[:, n * LANES : (n + 1) * LANES]
-            tables[layer][(j + 1) * across + i + 1] = part[:LANES].astype(BF16)
+            tables[layer][j + 1, i + 1] = part[:LANES].astype(BF16)
             pr[i * bins_y + j] = (part[LANES:] + columns[layer, 0]).astype(BF16)
 
-    def remote(layer, source, place, rows, slot, device):
+    def remote(layer, source, place, which):
         return pltpu.make_async_remote_copy(
-            src_ref=tables[layer].at[pl.ds(source, rows)],
-            dst_ref=tables[layer].at[pl.ds(place, rows)],
-            send_sem=halo_send.at[layer, slot],
-            recv_sem=halo_recv.at[layer, slot],
-            device_id=device,
+            src_ref=tables[layer].at[source],
+            dst_ref=tables[layer].at[place],
+            send_sem=halo_send.at[layer, which],
+            recv_sem=halo_recv.at[layer, which],
+            device_id=neighbour(*DIRECTIONS[which]),
             device_id_type=MESH,
         )
 
-    pairs = bins_x // 2
-
-    def column_copies(layer, n):
-        left = remote(
-            layer, across + 1 + 2 * n, (bins_y + 1) * across + 1 + 2 * n, 2, n, neighbour(0, -1)
-        )
-        right = remote(
-            layer, bins_y * across + 1 + 2 * n, 1 + 2 * n, 2, pairs + n, neighbour(0, 1)
-        )
-        return left, right
-
-    def other_copies(layer):
-        copies = []
-        slot = 2 * pairs
-        for step_x, step_y in ((-1, -1), (-1, 1), (1, -1), (1, 1)):
-            source = (1 if step_y < 0 else bins_y) * across + (1 if step_x < 0 else bins_x)
-            place = (bins_y + 1 if step_y < 0 else 0) * across + (
-                bins_x + 1 if step_x < 0 else 0
-            )
-            copies.append(remote(layer, source, place, 1, slot, neighbour(step_x, step_y)))
-            slot += 1
-        for step_x in (-1, 1):
-            for j in range(bins_y):
-                source = (j + 1) * across + (1 if step_x < 0 else bins_x)
-                place = (j + 1) * across + (bins_x + 1 if step_x < 0 else 0)
-                copies.append(remote(layer, source, place, 1, slot, neighbour(step_x, 0)))
-                slot += 1
-        return copies
+    def halo(layer, which, rows=None):
+        step_x, step_y = DIRECTIONS[which]
+        near_y, far_y = (1, bins_y + 1) if step_y < 0 else (bins_y, 0)
+        near_x, far_x = (1, bins_x + 1) if step_x < 0 else (bins_x, 0)
+        if step_x == 0:
+            rows = pl.ds(1, bins_x) if rows is None else rows
+            return remote(layer, (near_y, rows), (far_y, rows), which)
+        if step_y == 0:
+            columns_ = pl.ds(1, bins_y)
+            return remote(layer, (columns_, near_x), (columns_, far_x), which)
+        return remote(layer, (near_y, near_x), (far_y, far_x), which)
 
     def exchange(layer, renew):
+        left, right, low, high = 0, bins_y - 1, 0, bins_x - 1
+        cells = [(low, left), (high, left), (low, right), (high, right)]
+        place_tables(layer, cells, renew(cells))
+        for which in (0, 2, 5, 7):
+            halo(layer, which).start()
+        for which in (3, 4):
+            halo(layer, which, pl.ds(1 + low, 1)).start()
+            halo(layer, which, pl.ds(1 + high, 1)).start()
+        cells = [(i, j) for i in (low, high) for j in range(left + 1, right)]
+        place_tables(layer, cells, renew(cells))
+        for which in (1, 6):
+            halo(layer, which).start()
+
         def outer(n, _):
-            cells = [(2 * n, 0), (2 * n + 1, 0), (2 * n, bins_y - 1), (2 * n + 1, bins_y - 1)]
+            row = 2 * n + 1
+            cells = [(row, left), (row + 1, left), (row, right), (row + 1, right)]
             place_tables(layer, cells, renew(cells))
-            for copy in column_copies(layer, n):
-                copy.start()
+            for which in (3, 4):
+                halo(layer, which, pl.ds(1 + row, 2)).start()
             return 0
 
-        lax.fori_loop(0, pairs, outer, 0)
-        corners = other_copies(layer)
-        for copy in corners[:4]:
-            copy.start()
+        lax.fori_loop(0, bins_x // 2 - 1, outer, 0)
 
         def inner(n, _):
-            cells = [(2 * n, 1), (2 * n + 1, 1), (2 * n, 2), (2 * n + 1, 2)]
+            row = 2 * n + 1
+            cells = [(row + i, j) for i in range(2) for j in range(left + 1, right)]
             place_tables(layer, cells, renew(cells))
             return 0
 
-        lax.fori_loop(0, pairs, inner, 0)
-        for copy in corners[4:]:
-            copy.start()
+        lax.fori_loop(0, bins_x // 2 - 1, inner, 0)
 
     def finish_exchange(layer):
-        for copy in other_copies(layer):
-            copy.wait()
-        for n in range(pairs):
-            for copy in column_copies(layer, n):
-                copy.wait()
+        for which in range(8):
+            halo(layer, which).wait_recv()
+
+    plan_copy.wait()
+    for copy in edge_loads:
+        copy.wait()
+
+    def mark_tile(p, _):
+        t = plan[0, p]
+        from_row = es[pl.ds(t, 1), :]
+        to_row = er[pl.ds(t, 1), :]
+        hot[p, :LANES, :] = jnp.where(sub == from_row, 1.0, 0.0).astype(BF16)
+        to_hot = jnp.where(sub == to_row, 1.0, 0.0).astype(BF16)
+        hot[p, LANES:, :] = to_hot
+        hot_n[p] = (turned(identity, to_hot) * plan[4, p].astype(F32)).astype(BF16)
+        return 0
+
+    lax.fori_loop(0, EARLY, mark_tile, 0, unroll=8)
 
     for copy in mig_copies:
         copy.wait()
@@ -266,22 +275,11 @@
         return jnp.concatenate(values, axis=1)
 
     exchange(0, settle)
-
-    plan_copy.wait()
-    for copy in edge_loads:
-        copy.wait()
-
-    def mark_tile(p, _):
-        t = plan[0, p]
-        from_row = es[pl.ds(t, 1), :]
-        to_row = er[pl.ds(t, 1), :]
-        hot[p, :LANES, :] = jnp.where(sub == from_row, 1.0, 0.0).astype(BF16)
-        to_hot = jnp.where(sub == to_row, 1.0, 0.0).astype(BF16)
-        hot[p, LANES:, :] = to_hot
-        hot_n[p] = (turned(identity, to_hot) * plan[4, p].astype(F32)).astype(BF16)
+    lax.fori_loop(EARLY, tiles, mark_tile, 0, unroll=8)
+
+    def receivers_of(p, _):
+        to_rows[p] = dot(pr[plan[2, p]], hot[p, LANES:, :]).astype(BF16)
         return 0
-
-    lax.fori_loop(0, tiles, mark_tile, 0, unroll=8)
 
     def messages(layer):
         table = tables[layer]
@@ -290,8 +288,8 @@
             hidden = []
             for g in range(GROUP):
                 p = q * GROUP + g
-                both = jnp.concatenate([table[plan[1, p]], pr[plan[2, p]]], axis=1)
-                hidden.append(jnp.maximum(dot(both, hot[p]), 0.0).astype(BF16))
+                pre = dot(table[plan[1, p], plan[6, p]], hot[p, :LANES, :])
+                hidden.append(jnp.maximum(pre + to_rows[p].astype(F32), 0.0).astype(BF16))
             sent = []
             for g in range(0, GROUP, 2):
                 pair = dot(w_edge[layer], jnp.concatenate(hidden[g : g + 2], axis=1))
@@ -328,6 +326,7 @@
         return renew
 
     for layer in range(LAYERS):
+        lax.fori_loop(0, tiles, receivers_of, 0, unroll=16)
         finish_exchange(layer)
         messages(layer)
         if layer < LAYERS - 1:
@@ -336,16 +335,21 @@
             renew = node(layer)
 
             def final(n, _):
-                cells = [(n, j) for j in range(bins_y)]
+                cells = [(FINAL * n + i, j) for i in range(FINAL) for j in range(bins_y)]
                 new = renew(cells)
-                for j in range(bins_y):
-                    lat[n, j] = turned(identity, new[:, j * LANES : (j + 1) * LANES]).astype(BF16)
-                pltpu.make_async_copy(lat.at[n], out_ref.at[n], out_sem.at[n]).start()
+                for k, (i, j) in enumerate(cells):
+                    lat[i, j] = turned(identity, new[:, k * LANES : (k + 1) * LANES]).astype(BF16)
+                rows = pl.ds(FINAL * n, FINAL)
+                pltpu.make_async_copy(lat.at[rows], out_ref.at[rows], out_sem.at[n]).start()
                 return 0
 
-            lax.fori_loop(0, bins_x, final, 0)
-            for n in range(bins_x):
-                pltpu.make_async_copy(lat.at[n], out_ref.at[n], out_sem.at[n]).wait()
+            lax.fori_loop(0, bins_x // FINAL, final, 0)
+            for n in range(bins_x // FINAL):
+                rows = pl.ds(FINAL * n, FINAL)
+                pltpu.make_async_copy(lat.at[rows], out_ref.at[rows], out_sem.at[n]).wait()
+    for layer in range(LAYERS):
+        for which in range(8):
+            halo(layer, which).wait_send()
 
 
 def body(*arguments):
@@ -354,12 +358,11 @@
     tiles = tile_target.shape[2]
     mig = migration.shape[3]
     cells = bins_x * bins_y
-    table = (bins_x + 2) * (bins_y + 2)
+    table = (bins_y + 2, bins_x + 2)
     hbm = pl.BlockSpec(memory_space=pl.ANY)
     vmem = pl.BlockSpec(memory_space=pltpu.VMEM)
     smem = pl.BlockSpec(memory_space=pltpu.SMEM)
     block = (LANES, LANES)
-    halos = 2 * (bins_x // 2) + 4 + 2 * bins_y
     dma = pltpu.SemaphoreType.DMA
     return pl.pallas_call(
         kernel,
@@ -381,9 +384,10 @@
             pltpu.VMEM((tiles, LANES), jnp.int32),
             pltpu.VMEM((tiles, 2 * LANES, LANES), BF16),
             pltpu.VMEM((tiles,) + block, BF16),
-            pltpu.VMEM((table,) + block, BF16),
-            pltpu.VMEM((table,) + block, BF16),
-            pltpu.VMEM((table,) + block, BF16),
+            pltpu.VMEM((tiles,) + block, BF16),
+            pltpu.VMEM(table + block, BF16),
+            pltpu.VMEM(table + block, BF16),
+            pltpu.VMEM(table + block, BF16),
             pltpu.VMEM((cells,) + block, BF16),
             pltpu.VMEM((tiles + 1,) + block, BF16),
             pltpu.VMEM((cells,) + block, BF16),
@@ -399,8 +403,8 @@
             dma,
             dma((8,)),
             dma((8,)),
-            dma((LAYERS, halos)),
-            dma((LAYERS, halos)),
+            dma((LAYERS, 8)),
+            dma((LAYERS, 8)),
             dma((bins_x,)),
         ],
         compiler_params=pltpu.CompilerParams(

time: 75.4 us -> 62.7 us (0.83)
  the two profiles are of different devices: /device:TPU:0 before, /device:TPU:40 now
where the time goes in v1:
time: 62.7 us; the launch traced here: 62.5 us
  Pallas kernels  59.5 us (95%)
  local copies, waits for them, and re-layouts  2.31 us (4%)
  between operations  0.66 us (1%)
    pallas_call x1, Pallas kernels, body(): pl.pallas_call(kernel, out_shape=jax.ShapeDtypeStruct(latent.shape, laten...  59.5 us
    unnamed x1, local copies, waits for them, and re-layouts  2.31 us

profile of v1, /device:TPU:40, one launch (start us, length us, event | category | flops | bytes accessed | tf_op | source)
XLA Modules:
  0.0 62.5 jit_solution(13895096259170457561)
XLA Ops:
  0.7 59.5 %particles.1 = bf16[8,4,128,128]{3,2,1,0:T(8,128)(2,1)} custom-call(bf16[8,4,128,128]{3,2,1,0:T(8,128)(2,1)} %latent.1, s32[1,1,8,64]{3,2,1,0:T(8,128)} %mig_v.1, s32[1,1,8,64]{3,2,1,0:T(8,128)} %mig_v.1, s32[1,1,128]{2,1,0:T(1,128)} %target.1, s32[1,1,128]{2,1,0:T(1,128)} %offset.1, s32[1,1]{1,0:T(1,128)S(6)} %copy.19.count, s32[1,1,128,128]{3,2,1,0:T(8,128)} %senders.1, ...), custom_call_target="tpu_custom_call" | custom-call | tf_op jit(solution)/shard_map/particles/pallas_call | solution.py:367
  60.2 2.3 %copy.20 = bf16[8,4,128,128]{3,2,1,0:T(8,128)(2,1)} copy(bf16[8,4,128,128]{3,2,1,0:T(8,128)(2,1)} %particles.1) | data formatting | bytes 2097152

commit v2 on v1

--- a/solution.py
+++ b/solution.py
@@ -10,7 +10,7 @@
 F32 = jnp.float32
 BF16 = jnp.bfloat16
 LANES = 128
-GROUP = 32
+GROUP = 64
 LAYERS = 3
 EARLY = 64
 FINAL = 4
@@ -172,70 +172,89 @@
         columns[layer, 1] = spread(node_b[layer : layer + 1, :])
         columns[layer, 2] = spread(node_g[layer : layer + 1, :])
 
-    def place_tables(layer, cells, values):
-        both = dot(w_sr[layer], values)
-        for n, (i, j) in enumerate(cells):
-            part = both[:, n * LANES : (n + 1) * LANES]
-            tables[layer][j + 1, i + 1] = part[:LANES].astype(BF16)
-            pr[i * bins_y + j] = (part[LANES:] + columns[layer, 0]).astype(BF16)
-
-    def remote(layer, source, place, which):
+    def place_tables(layer, pairs, values):
+        bias = jnp.concatenate([columns[layer, 0]] * 2, axis=1)
+        for pair, value in zip(pairs, values):
+            both = dot(w_sr[layer], value)
+            sending = both[:LANES].astype(BF16)
+            receiving = (both[LANES:] + bias).astype(BF16)
+            for n, (i, j) in enumerate(pair):
+                part = slice(n * LANES, (n + 1) * LANES)
+                tables[layer][j + 1, i + 1] = sending[:, part]
+                pr[i * bins_y + j] = receiving[:, part]
+
+    def remote(layer, source, place, device, slot):
         return pltpu.make_async_remote_copy(
             src_ref=tables[layer].at[source],
             dst_ref=tables[layer].at[place],
-            send_sem=halo_send.at[layer, which],
-            recv_sem=halo_recv.at[layer, which],
-            device_id=neighbour(*DIRECTIONS[which]),
+            send_sem=halo_send.at[layer, slot],
+            recv_sem=halo_recv.at[layer, slot],
+            device_id=device,
             device_id_type=MESH,
         )
 
-    def halo(layer, which, rows=None):
-        step_x, step_y = DIRECTIONS[which]
-        near_y, far_y = (1, bins_y + 1) if step_y < 0 else (bins_y, 0)
-        near_x, far_x = (1, bins_x + 1) if step_x < 0 else (bins_x, 0)
-        if step_x == 0:
-            rows = pl.ds(1, bins_x) if rows is None else rows
-            return remote(layer, (near_y, rows), (far_y, rows), which)
-        if step_y == 0:
-            columns_ = pl.ds(1, bins_y)
-            return remote(layer, (columns_, near_x), (columns_, far_x), which)
-        return remote(layer, (near_y, near_x), (far_y, far_x), which)
+    def column(layer, step_y, row, rows, slot):
+        near, far = (1, bins_y + 1) if step_y < 0 else (bins_y, 0)
+        cells = pl.ds(1 + row, rows)
+        return remote(layer, (near, cells), (far, cells), neighbour(0, step_y), slot)
+
+    def line(layer, step_x):
+        near, far = (1, bins_x + 1) if step_x < 0 else (bins_x, 0)
+        cells = pl.ds(1, bins_y)
+        return remote(layer, (cells, near), (cells, far), neighbour(step_x, 0), 4 + (step_x > 0))
+
+    odd = lax.rem(a, 2)
+
+    def outer_corner(layer, step_y):
+        near, far = (1, bins_y + 1) if step_y < 0 else (bins_y, 0)
+        source = 1 + (bins_x - 1) * odd
+        place = (bins_x + 1) * (1 - odd)
+        device = neighbour(2 * odd - 1, step_y)
+        return remote(layer, (near, source), (far, place), device, 6 + (step_y > 0))
+
+    def passed_corner(layer, far):
+        source = bins_x - (bins_x - 1) * odd
+        place = (bins_x + 1) * odd
+        device = neighbour(1 - 2 * odd, 0)
+        return remote(layer, (far, source), (far, place), device, 8 + (far > 0))
+
+    left, right, low, high = 0, bins_y - 1, 0, bins_x - 1
+    middle = [(i, j) for i in range(low + 1, high) for j in range(left + 1, right)]
+
+    def in_pairs(cells):
+        return [cells[k : k + 2] for k in range(0, len(cells), 2)]
 
     def exchange(layer, renew):
-        left, right, low, high = 0, bins_y - 1, 0, bins_x - 1
-        cells = [(low, left), (high, left), (low, right), (high, right)]
-        place_tables(layer, cells, renew(cells))
-        for which in (0, 2, 5, 7):
-            halo(layer, which).start()
-        for which in (3, 4):
-            halo(layer, which, pl.ds(1 + low, 1)).start()
-            halo(layer, which, pl.ds(1 + high, 1)).start()
-        cells = [(i, j) for i in (low, high) for j in range(left + 1, right)]
-        place_tables(layer, cells, renew(cells))
-        for which in (1, 6):
-            halo(layer, which).start()
-
-        def outer(n, _):
-            row = 2 * n + 1
-            cells = [(row, left), (row + 1, left), (row, right), (row + 1, right)]
-            place_tables(layer, cells, renew(cells))
-            for which in (3, 4):
-                halo(layer, which, pl.ds(1 + row, 2)).start()
-            return 0
-
-        lax.fori_loop(0, bins_x // 2 - 1, outer, 0)
-
-        def inner(n, _):
-            row = 2 * n + 1
-            cells = [(row + i, j) for i in range(2) for j in range(left + 1, right)]
-            place_tables(layer, cells, renew(cells))
-            return 0
-
-        lax.fori_loop(0, bins_x // 2 - 1, inner, 0)
+        pairs = in_pairs([(low, left), (high, left), (low, right), (high, right)])
+        place_tables(layer, pairs, renew(pairs))
+        for side, step_y in enumerate((-1, 1)):
+            outer_corner(layer, step_y).start()
+            column(layer, step_y, low, 1, side).start()
+            column(layer, step_y, high, 1, side).start()
+        pairs = in_pairs([(i, j) for i in (low, high) for j in range(left + 1, right)])
+        pairs += in_pairs([(i, j) for j in (left, right) for i in range(low + 1, high)])
+        place_tables(layer, pairs, renew(pairs))
+        for step_x in (-1, 1):
+            line(layer, step_x).start()
+        for side, step_y in enumerate((-1, 1)):
+            column(layer, step_y, low + 1, bins_x - 2, 2 + side).start()
+        pairs = in_pairs(middle)
+        place_tables(layer, pairs, renew(pairs))
+        for side, step_y in enumerate((-1, 1)):
+            column(layer, step_y, low, 2, side).wait_recv()
+        for far in (0, bins_y + 1):
+            passed_corner(layer, far).start()
+
+    def halo_waits(layer):
+        copies = [line(layer, step_x) for step_x in (-1, 1)]
+        copies += [outer_corner(layer, step_y) for step_y in (-1, 1)]
+        copies += [passed_corner(layer, far) for far in (0, bins_y + 1)]
+        copies += [column(layer, (-1, 1)[side], 1, bins_x - 2, 2 + side) for side in range(2)]
+        return copies
 
     def finish_exchange(layer):
-        for which in range(8):
-            halo(layer, which).wait_recv()
+        for copy in halo_waits(layer):
+            copy.wait_recv()
 
     plan_copy.wait()
     for copy in edge_loads:
@@ -244,14 +263,17 @@
     def mark_tile(p, _):
         t = plan[0, p]
         from_row = es[pl.ds(t, 1), :]
-        to_row = er[pl.ds(t, 1), :]
+        to_row = jnp.where(plan[4, p] > 0, er[pl.ds(t, 1), :], -1)
         hot[p, :LANES, :] = jnp.where(sub == from_row, 1.0, 0.0).astype(BF16)
         to_hot = jnp.where(sub == to_row, 1.0, 0.0).astype(BF16)
         hot[p, LANES:, :] = to_hot
-        hot_n[p] = (turned(identity, to_hot) * plan[4, p].astype(F32)).astype(BF16)
+        hot_n[p] = turned(identity, to_hot).astype(BF16)
         return 0
 
-    lax.fori_loop(0, EARLY, mark_tile, 0, unroll=8)
+    lax.fori_loop(0, EARLY, mark_tile, 0, unroll=16)
+
+    def together(table, pair):
+        return jnp.concatenate([table[i * bins_y + j] for i, j in pair], axis=1)
 
     for copy in mig_copies:
         copy.wait()
@@ -262,20 +284,20 @@
         ).astype(BF16)
     arrived_t[LANES:, :] = jnp.ones((16, 4 * LANES), BF16)
 
-    def settle(cells):
+    def settle(pairs):
         values = []
-        for i, j in cells:
-            n = i * bins_y + j
-            placed = dot(arrived_t[...], mig_hot[n])
-            new = jnp.where(
-                placed[LANES : LANES + 1] > 0.5, placed[:LANES], state[n].astype(F32)
-            ).astype(BF16)
-            state[n] = new
-            values.append(new)
-        return jnp.concatenate(values, axis=1)
+        for pair in pairs:
+            for i, j in pair:
+                n = i * bins_y + j
+                placed = dot(arrived_t[...], mig_hot[n])
+                state[n] = jnp.where(
+                    placed[LANES : LANES + 1] > 0.5, placed[:LANES], state[n].astype(F32)
+                ).astype(BF16)
+            values.append(together(state, pair))
+        return values
 
     exchange(0, settle)
-    lax.fori_loop(EARLY, tiles, mark_tile, 0, unroll=8)
+    lax.fori_loop(EARLY, tiles, mark_tile, 0, unroll=16)
 
     def receivers_of(p, _):
         to_rows[p] = dot(pr[plan[2, p]], hot[p, LANES:, :]).astype(BF16)
@@ -305,23 +327,26 @@
         lax.fori_loop(0, tiles // GROUP, group, jnp.zeros((LANES, LANES), F32))
 
     def node(layer):
-        def renew(cells):
-            old = jnp.concatenate([state[i * bins_y + j] for i, j in cells], axis=1)
-            summed = jnp.concatenate(
-                [sums[plan[5, i * bins_y + j]] for i, j in cells], axis=1
-            )
-            many = len(cells)
-            bias = jnp.concatenate([columns[layer, 1]] * many, axis=1)
-            gain = jnp.concatenate([columns[layer, 2]] * many, axis=1)
-            hidden = dot(w_node[layer], jnp.concatenate([old, summed], axis=0)) + bias
-            hidden = jnp.maximum(hidden, 0.0).astype(BF16)
-            z = dot(w_out[layer], hidden)
-            var = jnp.mean(z * z, axis=0, keepdims=True)
-            new = (old.astype(F32) + z * lax.rsqrt(var + 1e-5) * gain).astype(BF16)
+        def renew(pairs):
+            bias = jnp.concatenate([columns[layer, 1]] * 2, axis=1)
+            gain = jnp.concatenate([columns[layer, 2]] * 2, axis=1)
+            hidden = []
+            for pair in pairs:
+                summed = jnp.concatenate([sums[plan[5, i * bins_y + j]] for i, j in pair], axis=1)
+                both = jnp.concatenate([together(state, pair), summed], axis=0)
+                pre = dot(w_node[layer], both) + bias
+                hidden.append(jnp.maximum(pre, 0.0).astype(BF16))
+            values = []
+            for pair, value in zip(pairs, hidden):
+                z = dot(w_out[layer], value)
+                var = jnp.mean(z * z, axis=0, keepdims=True)
+                step = z * lax.rsqrt(var + 1e-5) * gain
+                values.append((together(state, pair).astype(F32) + step).astype(BF16))
             if layer < LAYERS - 1:
-                for n, (i, j) in enumerate(cells):
-                    state[i * bins_y + j] = new[:, n * LANES : (n + 1) * LANES]
-            return new
+                for pair, value in zip(pairs, values):
+                    for n, (i, j) in enumerate(pair):
+                        state[i * bins_y + j] = value[:, n * LANES : (n + 1) * LANES]
+            return values
 
         return renew
 
@@ -334,22 +359,27 @@
         else:
             renew = node(layer)
 
-            def final(n, _):
-                cells = [(FINAL * n + i, j) for i in range(FINAL) for j in range(bins_y)]
-                new = renew(cells)
-                for k, (i, j) in enumerate(cells):
-                    lat[i, j] = turned(identity, new[:, k * LANES : (k + 1) * LANES]).astype(BF16)
+            outs = []
+            for n in range(bins_x // FINAL):
+                pairs = in_pairs(
+                    [(FINAL * n + i, j) for i in range(FINAL) for j in range(bins_y)]
+                )
+                for pair, value in zip(pairs, renew(pairs)):
+                    for k, (i, j) in enumerate(pair):
+                        part = value[:, k * LANES : (k + 1) * LANES]
+                        lat[i, j] = part
                 rows = pl.ds(FINAL * n, FINAL)
-                pltpu.make_async_copy(lat.at[rows], out_ref.at[rows], out_sem.at[n]).start()
-                return 0
-
-            lax.fori_loop(0, bins_x // FINAL, final, 0)
-            for n in range(bins_x // FINAL):
-                rows = pl.ds(FINAL * n, FINAL)
-                pltpu.make_async_copy(lat.at[rows], out_ref.at[rows], out_sem.at[n]).wait()
+                outs.append(
+                    pltpu.make_async_copy(lat.at[rows], out_ref.at[rows], out_sem.at[n])
+                )
+                outs[-1].start()
+            for copy in outs:
+                copy.wait()
     for layer in range(LAYERS):
-        for which in range(8):
-            halo(layer, which).wait_send()
+        for copy in halo_waits(layer):
+            copy.wait_send()
+        for side, step_y in enumerate((-1, 1)):
+            column(layer, step_y, 0, 2, side).wait_send()
 
 
 def body(*arguments):
@@ -364,7 +394,7 @@
     smem = pl.BlockSpec(memory_space=pltpu.SMEM)
     block = (LANES, LANES)
     dma = pltpu.SemaphoreType.DMA
-    return pl.pallas_call(
+    turned_result = pl.pallas_call(
         kernel,
         out_shape=jax.ShapeDtypeStruct(latent.shape, latent.dtype),
         in_specs=[
@@ -403,8 +433,8 @@
             dma,
             dma((8,)),
             dma((8,)),
-            dma((LAYERS, 8)),
-            dma((LAYERS, 8)),
+            dma((LAYERS, 10)),
+            dma((LAYERS, 10)),
             dma((bins_x,)),
         ],
         compiler_params=pltpu.CompilerParams(
@@ -412,6 +442,7 @@
         ),
         name="particles",
     )(arguments[0], migration, *arguments[1:])
+    return jnp.swapaxes(turned_result, 2, 3)
 
 
 def solution(mesh):

time: 62.7 us -> 59.1 us (0.943)
  the two profiles are of different devices: /device:TPU:40 before, /device:TPU:0 now
where the time goes in v2:
time: 59.1 us; the launch traced here: 58.9 us
  Pallas kernels  56 us (95%)
  local copies, waits for them, and re-layouts  2.27 us (4%)
  between operations  0.66 us (1%)
    pallas_call x1, Pallas kernels, body(): pl.pallas_call(kernel, out_shape=jax.ShapeDtypeStruct(latent.shape, laten...  56 us
    transpose x1, local copies, waits for them, and re-layouts, body(): return jnp.swapaxes(turned_result, 2, 3)  2.27 us

profile of v2, /device:TPU:0, one launch (start us, length us, event | category | flops | bytes accessed | tf_op | source)
XLA Modules:
  0.0 58.9 jit_solution(9379829074060917670)
XLA Ops:
  0.7 56.0 %particles.1 = bf16[8,4,128,128]{3,2,1,0:T(8,128)(2,1)} custom-call(bf16[8,4,128,128]{3,2,1,0:T(8,128)(2,1)} %latent.1, s32[1,1,8,64]{3,2,1,0:T(8,128)} %mig_v.1, s32[1,1,8,64]{3,2,1,0:T(8,128)} %mig_v.1, s32[1,1,128]{2,1,0:T(1,128)} %target.1, s32[1,1,128]{2,1,0:T(1,128)} %offset.1, s32[1,1]{1,0:T(1,128)S(6)} %copy.19.count, s32[1,1,128,128]{3,2,1,0:T(8,128)} %senders.1, ...), custom_call_target="tpu_custom_call" | custom-call | tf_op jit(solution)/shard_map/particles/pallas_call | solution.py:397
  56.7 2.3 %copy.18 = bf16[8,4,128,128]{3,2,1,0:T(8,128)(2,1)} copy(bf16[8,4,128,128]{2,3,1,0:T(8,128)(2,1)} %bitcast.1) | data formatting | bytes 2097152 | tf_op jit(solution)/shard_map/transpose | solution.py:445

commit v3 on v2

--- a/solution.py
+++ b/solution.py
@@ -68,19 +68,20 @@
         lat32[pl.ds(n * LANES, LANES), :] = lat[n // bins_y, n % bins_y].astype(F32)
         return 0
 
-    lax.fori_loop(0, bins_x * bins_y, widen, 0, unroll=4)
+    lax.fori_loop(0, bins_x * bins_y, widen, 0, unroll=8)
 
     pl.semaphore_wait(barrier, 8)
 
     mig = mig_s.shape[3]
     mig_copies = []
-    for which, (step_x, step_y) in enumerate(DIRECTIONS):
+    for which in (0, 2, 5, 7, 1, 6, 3, 4):
+        step_x, step_y = DIRECTIONS[which]
 
         def pick(m, _, which=which):
             stage[pl.ds(m, 1), :] = lat32[pl.ds(mig_s[0, 0, which, m], 1), :]
             return 0
 
-        lax.fori_loop(0, mig, pick, 0, unroll=16)
+        lax.fori_loop(0, mig, pick, 0, unroll=32)
         parcels[which] = stage[...].astype(BF16)
         copy = pltpu.make_async_remote_copy(
             src_ref=parcels.at[which],
@@ -113,13 +114,13 @@
             ).astype(BF16)
             return 0
 
-        lax.fori_loop(0, bins_x * bins_y, mark, 0, unroll=4)
+        lax.fori_loop(0, bins_x * bins_y, mark, 0, unroll=16)
 
     def turn(n, _):
         state[n] = turned(identity, lat[n // bins_y, n % bins_y]).astype(BF16)
         return 0
 
-    lax.fori_loop(0, bins_x * bins_y, turn, 0, unroll=8)
+    lax.fori_loop(0, bins_x * bins_y, turn, 0, unroll=32)
 
     lane_row = lax.broadcasted_iota(jnp.int32, (1, LANES), 1)
     bin_row = target[0, 0:1, :]
@@ -270,7 +271,7 @@
         hot_n[p] = turned(identity, to_hot).astype(BF16)
         return 0
 
-    lax.fori_loop(0, EARLY, mark_tile, 0, unroll=16)
+    lax.fori_loop(0, EARLY, mark_tile, 0, unroll=32)
 
     def together(table, pair):
         return jnp.concatenate([table[i * bins_y + j] for i, j in pair], axis=1)
@@ -297,7 +298,7 @@
         return values
 
     exchange(0, settle)
-    lax.fori_loop(EARLY, tiles, mark_tile, 0, unroll=16)
+    lax.fori_loop(EARLY, tiles, mark_tile, 0, unroll=32)
 
     def receivers_of(p, _):
         to_rows[p] = dot(pr[plan[2, p]], hot[p, LANES:, :]).astype(BF16)
@@ -351,7 +352,7 @@
         return renew
 
     for layer in range(LAYERS):
-        lax.fori_loop(0, tiles, receivers_of, 0, unroll=16)
+        lax.fori_loop(0, tiles, receivers_of, 0, unroll=64)
         finish_exchange(layer)
         messages(layer)
         if layer < LAYERS - 1:

time: 59.1 us -> 57.4 us (0.971)
  Pallas kernels: 56 us -> 54.3 us
    pallas_call x1, Pallas kernels: 56 us -> 54.3 us  [body(): pl.pallas_call(kernel, out_shape=jax.ShapeDtypeStruct(latent.shape, laten...]
where the time goes in v3:
time: 57.4 us; the launch traced here: 57.2 us
  Pallas kernels  54.3 us (95%)
  local copies, waits for them, and re-layouts  2.27 us (4%)
  between operations  0.66 us (1%)
    pallas_call x1, Pallas kernels, body(): pl.pallas_call(kernel, out_shape=jax.ShapeDtypeStruct(latent.shape, laten...  54.3 us
    transpose x1, local copies, waits for them, and re-layouts, body(): return jnp.swapaxes(turned_result, 2, 3)  2.27 us

profile of v3, /device:TPU:0, one launch (start us, length us, event | category | flops | bytes accessed | tf_op | source)
XLA Modules:
  0.0 57.2 jit_solution(8635120995850121215)
XLA Ops:
  0.7 54.3 %particles.1 = bf16[8,4,128,128]{3,2,1,0:T(8,128)(2,1)} custom-call(bf16[8,4,128,128]{3,2,1,0:T(8,128)(2,1)} %latent.1, s32[1,1,8,64]{3,2,1,0:T(8,128)} %mig_v.1, s32[1,1,8,64]{3,2,1,0:T(8,128)} %mig_v.1, s32[1,1,128]{2,1,0:T(1,128)} %target.1, s32[1,1,128]{2,1,0:T(1,128)} %offset.1, s32[1,1]{1,0:T(1,128)S(6)} %copy.19.count, s32[1,1,128,128]{3,2,1,0:T(8,128)} %senders.1, ...), custom_call_target="tpu_custom_call" | custom-call | tf_op jit(solution)/shard_map/particles/pallas_call | solution.py:398
  54.9 2.3 %copy.18 = bf16[8,4,128,128]{3,2,1,0:T(8,128)(2,1)} copy(bf16[8,4,128,128]{2,3,1,0:T(8,128)(2,1)} %bitcast.1) | data formatting | bytes 2097152 | tf_op jit(solution)/shard_map/transpose | solution.py:446

commit v4 on v3

--- a/solution.py
+++ b/solution.py
@@ -43,8 +43,15 @@
     def neighbour(step_x, step_y):
         return (lax.rem(a + step_x + count_a, count_a), lax.rem(b + step_y + count_b, count_b))
 
-    lat_copy = pltpu.make_async_copy(latent, lat, in_sem.at[0])
-    lat_copy.start()
+    parts = bins_x // 4
+    lat_copies = [
+        pltpu.make_async_copy(
+            latent.at[pl.ds(n * parts, parts)], lat.at[pl.ds(n * parts, parts)], in_sem.at[9 + n]
+        )
+        for n in range(4)
+    ]
+    for copy in lat_copies:
+        copy.start()
     loads = [
         pltpu.make_async_copy(source, raw.at[which], in_sem.at[1 + which])
         for which, source in enumerate((send_w, recv_w, edge_w, node_w, agg_w, out_w))
@@ -62,13 +69,14 @@
             barrier, inc=1, device_id=neighbour(step_x, step_y), device_id_type=MESH
         )
 
-    lat_copy.wait()
-
     def widen(n, _):
         lat32[pl.ds(n * LANES, LANES), :] = lat[n // bins_y, n % bins_y].astype(F32)
         return 0
 
-    lax.fori_loop(0, bins_x * bins_y, widen, 0, unroll=8)
+    for n, copy in enumerate(lat_copies):
+        copy.wait()
+        each = parts * bins_y
+        lax.fori_loop(n * each, (n + 1) * each, widen, 0, unroll=8)
 
     pl.semaphore_wait(barrier, 8)
 
@@ -374,13 +382,13 @@
                     pltpu.make_async_copy(lat.at[rows], out_ref.at[rows], out_sem.at[n])
                 )
                 outs[-1].start()
+            for past in range(LAYERS):
+                for copy in halo_waits(past):
+                    copy.wait_send()
+                for side, step_y in enumerate((-1, 1)):
+                    column(past, step_y, 0, 2, side).wait_send()
             for copy in outs:
                 copy.wait()
-    for layer in range(LAYERS):
-        for copy in halo_waits(layer):
-            copy.wait_send()
-        for side, step_y in enumerate((-1, 1)):
-            column(layer, step_y, 0, 2, side).wait_send()
 
 
 def body(*arguments):
@@ -430,7 +438,7 @@
             pltpu.VMEM((6, LAYERS) + block, BF16),
             pltpu.VMEM((8, LANES), jnp.int32),
             pltpu.SMEM((8, LANES), jnp.int32),
-            dma((9,)),
+            dma((13,)),
             dma,
             dma((8,)),
             dma((8,)),

time: 57.4 us -> 57.4 us (level)
  no operation moved by 1% of the time
where the time goes in v4:
time: 57.4 us; the launch traced here: 57.2 us
  Pallas kernels  54.2 us (94%)
  local copies, waits for them, and re-layouts  2.27 us (4%)
  between operations  0.66 us (1%)
    pallas_call x1, Pallas kernels, body(): pl.pallas_call(kernel, out_shape=jax.ShapeDtypeStruct(latent.shape, laten...  54.2 us
    transpose x1, local copies, waits for them, and re-layouts, body(): return jnp.swapaxes(turned_result, 2, 3)  2.27 us

profile of v4, /device:TPU:0, one launch (start us, length us, event | category | flops | bytes accessed | tf_op | source)
XLA Modules:
  0.0 57.2 jit_solution(5049953042095665053)
XLA Ops:
  0.7 54.2 %particles.1 = bf16[8,4,128,128]{3,2,1,0:T(8,128)(2,1)} custom-call(bf16[8,4,128,128]{3,2,1,0:T(8,128)(2,1)} %latent.1, s32[1,1,8,64]{3,2,1,0:T(8,128)} %mig_v.1, s32[1,1,8,64]{3,2,1,0:T(8,128)} %mig_v.1, s32[1,1,128]{2,1,0:T(1,128)} %target.1, s32[1,1,128]{2,1,0:T(1,128)} %offset.1, s32[1,1]{1,0:T(1,128)S(6)} %copy.19.count, s32[1,1,128,128]{3,2,1,0:T(8,128)} %senders.1, ...), custom_call_target="tpu_custom_call" | custom-call | tf_op jit(solution)/shard_map/particles/pallas_call | solution.py:406
  54.9 2.3 %copy.18 = bf16[8,4,128,128]{3,2,1,0:T(8,128)(2,1)} copy(bf16[8,4,128,128]{2,3,1,0:T(8,128)(2,1)} %bitcast.1) | data formatting | bytes 2097152 | tf_op jit(solution)/shard_map/transpose | solution.py:454
